TPU v7x, 256 devices: a whole 4x4x8 slice. The times are simulated.
256 devices in a mesh: dp: 2 (over y_hi), tensor: 8 (over z), passage: 16 (over x, y_lo, core).
Axes of the slice: x: 4, y: 4 (y_hi: 2, y_lo: 2; y = y_hi * 2 + y_lo), z: 8, core: 2. Of those that a mesh axis runs over, the one named last changes fastest.
Arguments:
- answer_states: bfloat16 [2048, 4096], P(('dp', 'passage')), parts along dimension 0, may hold values from -6 to 6
- cross_keys: bfloat16 [32768, 4096], P(('dp', 'passage'), 'tensor'), parts along dimension 0, may hold values from -40 to 40
- cross_values: bfloat16 [32768, 4096], P(('dp', 'passage'), 'tensor'), parts along dimension 0, may hold values from -6 to 6
- passage_lengths: int32 [128], P(('dp', 'passage')), parts along dimension 0, may hold values from 32 to 256, as said below
- passage_sources: int32 [128], P(('dp', 'passage')), parts along dimension 0, may hold values from 0 to 31
- source_bias: float32 [32, 64], P(None, 'tensor'), may hold values from -4 to 4
- query_weight: bfloat16 [4096, 4096], P(None, 'tensor'), may hold values from -0.09375 to 0.09375
- output_weight: bfloat16 [4096, 4096], P('tensor'), may hold values from -0.09375 to 0.09375
- attn_gain: float32 [4096], replicated, may hold values from 0.5 to 1.5
- ffn_gain: float32 [4096], replicated, may hold values from 0.5 to 1.5
- gate_weight: bfloat16 [4096, 10240], P(None, ('tensor', 'passage')), may hold values from -0.09375 to 0.09375
- up_weight: bfloat16 [4096, 10240], P(None, ('tensor', 'passage')), may hold values from -0.09375 to 0.09375
- down_weight: bfloat16 [10240, 4096], P(('tensor', 'passage')), may hold values from -0.0625 to 0.0625
Outputs:
- block_out: bfloat16 [2048, 4096], P(('dp', 'passage'), 'tensor'), parts along dimension 0
There are 2 independent parts, one for each index of `dp`. A program takes and returns all parts, laid end to end along the dimension named above; an argument that names none is the same for every part. Nothing has to cross between parts.
Inputs may be any that keep to these rules, and one draw needn't show every extreme that they name: Each passage's leading passage_lengths slots are its tokens and the rest is padding; some passage of every query is full.
All inputs are finite; a program needn't handle non-finite values.
Results may differ from a plain program's by a relative error of at most 0.0075.
Values may be sent and summed in bfloat16 or wider, within the bound.
A program may use at most 128 MiB of HBM per device.

v0:
```python
import jax
import jax.numpy as jnp
from jax import lax
from jax.sharding import PartitionSpec as P

PLEN = 256
NB = 32


def joined_2(array, axis, combine):
    everything = jax.tree.map(lambda part: lax.all_gather(part, axis), array)
    leading = jax.tree.map(lambda part: part[0], everything)

    def turn(k, so_far):
        return combine(so_far, jax.tree.map(lambda part: part[k], everything))

    return lax.fori_loop(1, lax.axis_size(axis), turn, leading)


def rms_scale(values, gain):
    return values * lax.rsqrt(jnp.mean(values * values, axis=-1, keepdims=True) + 1e-06) * gain


def joined(first, second):
    out_first, peak_first, total_first = first
    out_second, peak_second, total_second = second
    highest = jnp.maximum(peak_first, peak_second)
    scale_first = jnp.exp(peak_first - highest)
    scale_second = jnp.exp(peak_second - highest)
    rows, head_count = peak_first.shape
    combined = (
        out_first.reshape(rows, head_count, -1) * scale_first[..., None]
        + out_second.reshape(rows, head_count, -1) * scale_second[..., None]
    )
    return (
        combined.reshape(out_first.shape),
        highest,
        total_first * scale_first + total_second * scale_second,
    )


def on_device(
    answer_states,
    cross_keys,
    cross_values,
    passage_lengths,
    passage_sources,
    source_bias,
    query_weight,
    output_weight,
    attn_gain,
    ffn_gain,
    gate_weight,
    up_weight,
    down_weight,
):
    tok_rows, width = answer_states.shape
    head_count = source_bias.shape[1]
    inner = query_weight.shape[1]
    head_size = inner // head_count
    states = answer_states.astype(jnp.float32)
    normed = rms_scale(states, attn_gain).astype(jnp.bfloat16)
    query_part = jnp.dot(normed, query_weight, preferred_element_type=jnp.float32).astype(
        jnp.bfloat16
    )
    query_all = lax.all_gather(query_part, "passage", axis=0, tiled=True)
    total_rows = query_all.shape[0]
    key_rows = cross_keys.shape[0]
    onehot = (passage_sources[:, None] == jnp.arange(NB, dtype=jnp.int32)[None, :]).astype(
        jnp.float32
    )
    per_passage = jnp.dot(onehot, source_bias, precision=lax.Precision.HIGHEST)
    key_bias = jnp.repeat(per_passage, PLEN, axis=0, total_repeat_length=key_rows).T
    valid = jnp.arange(key_rows, dtype=jnp.int32) % PLEN < jnp.repeat(
        passage_lengths, PLEN, total_repeat_length=key_rows
    )
    keys_split = cross_keys.reshape(key_rows, head_count, head_size)
    values_split = cross_values.reshape(key_rows, head_count, head_size)
    block_rows = min(total_rows, 512)
    blocks = query_all.reshape(total_rows // block_rows, block_rows, head_count, head_size)

    def attend(query_block):
        scores = jnp.einsum(
            "qhd,khd->hqk", query_block, keys_split, preferred_element_type=jnp.float32
        )
        scores = jnp.where(valid[None, None, :], scores + key_bias[:, None, :], jnp.float32(-1e30))
        peaks = jnp.max(scores, axis=-1)
        weights = jnp.exp(scores - peaks[..., None])
        totals = jnp.sum(weights, axis=-1)
        outputs = jnp.einsum(
            "hqk,khd->qhd",
            weights.astype(jnp.bfloat16),
            values_split,
            preferred_element_type=jnp.float32,
        )
        return (outputs.reshape(block_rows, inner), peaks.T, totals.T)

    outputs, maxima, sums = lax.map(attend, blocks)
    outputs = outputs.reshape(total_rows, inner)
    maxima = maxima.reshape(total_rows, head_count)
    sums = sums.reshape(total_rows, head_count)
    merged_out, merged_peak, merged_total = joined_2((outputs, maxima, sums), "passage", joined)
    start_row = lax.axis_index("passage") * tok_rows
    mine_out = lax.dynamic_slice_in_dim(merged_out, start_row, tok_rows, 0)
    mine_total = lax.dynamic_slice_in_dim(merged_total, start_row, tok_rows, 0)
    attended = (
        (mine_out.reshape(tok_rows, head_count, head_size) / mine_total[..., None])
        .reshape(tok_rows, inner)
        .astype(jnp.bfloat16)
    )
    projected = jnp.dot(attended, output_weight, preferred_element_type=jnp.float32)
    middle = states + lax.psum(projected, "tensor")
    ffn_in = rms_scale(middle, ffn_gain).astype(jnp.bfloat16)
    tensor_count = lax.axis_size("tensor")
    column_count = width // tensor_count
    piece = lax.all_gather(ffn_in, "passage", axis=0, tiled=True)
    gate = jnp.dot(piece, gate_weight, preferred_element_type=jnp.float32)
    upper = jnp.dot(piece, up_weight, preferred_element_type=jnp.float32)
    hidden_units = (jax.nn.gelu(gate, approximate=True) * upper).astype(jnp.bfloat16)
    row_sums = lax.psum_scatter(
        jnp.dot(hidden_units, down_weight, preferred_element_type=jnp.float32),
        "passage",
        scatter_dimension=0,
        tiled=True,
    )
    ffn_out = lax.psum_scatter(row_sums, "tensor", scatter_dimension=1, tiled=True)
    residual_cols = lax.dynamic_slice_in_dim(
        middle, lax.axis_index("tensor") * column_count, column_count, 1
    )
    return (residual_cols + ffn_out).astype(jnp.bfloat16)


def solution(mesh):
    return jax.shard_map(
        on_device,
        mesh=mesh,
        in_specs=(
            P(("dp", "passage"), None),
            P(("dp", "passage"), "tensor"),
            P(("dp", "passage"), "tensor"),
            P(("dp", "passage")),
            P(("dp", "passage")),
            P(None, "tensor"),
            P(None, "tensor"),
            P("tensor", None),
            P(),
            P(),
            P(None, ("tensor", "passage")),
            P(None, ("tensor", "passage")),
            P(("tensor", "passage"), None),
        ),
        out_specs=P(("dp", "passage"), "tensor"),
        check_vma=False,
    )
```

profile of v0, /device:TPU:1, one launch (start us, length us, event | category | flops | bytes accessed | tf_op | source)
XLA Modules:
  0.0 801.6 jit_solution(4265144462102150827)
XLA Ops:
  7.9 3.9 convolution_convert_fusion
  19.5 31.6 %all-gather.4.cloned.1.call-done = bf16[1024,512]{1,0:T(8,128)(2,1)} async-done(((bf16[64,512]{1,0:T(8,128)(2,1)}), bf16[1024,512]{1,0:T(8,128)(2,1)}) %all-gather.4.cloned.1.call-update) | async-done | bytes 1048592 | tf_op jit(solution)/shard_map/all_gather | solution.py:66
  51.1 3.9 reshape.166
  55.0 3.3 copy.29
  58.4 35.1 %while.37 = (s32[]{:T(128)}, f32[2,512,512]{2,1,0:T(8,128)}, f32[2,512,8]{1,2,0:T(8,128)S(1)}, f32[2,512,8]{1,2,0:T(8,128)S(1)}, bf16[2,512,8,64]{1,3,2,0:T(8,12...) while((s32[]{:T(128)}, f32[2,512,512]{2,1,0:T(8,128)}, ...), condition=%wide.region_4.5_spmd.clone, body=%wide.region_1.4_spmd.clone.sunk | while | flops 1119881216 | bytes 62628036 | solution.py:98
  60.9 3.5 fusion.77
  64.5 4.0 fusion.79
  68.5 4.8 fusion.78
  78.5 3.5 fusion.77
  82.0 4.0 fusion.79
  86.1 4.8 fusion.78
  93.5 19.6 %all_gather.18 = f32[16,1024,8]{1,2,0:T(8,128)S(1)} all-gather(f32[1,1024,8]{1,2,0:T(8,128)S(1)} %bitcast.92), channel_id=1, replica_groups=mesh['dp'=2,'tensor'=8,'passage'=16] {'passage'}, dimensions={0}, use_global_device_ids=true | all-gather | bytes 557056 | tf_op jit(solution)/shard_map/all_gather | solution.py:11
  114.0 18.9 %all_gather.17 = f32[16,1024,8]{1,2,0:T(8,128)S(1)} all-gather(f32[1,1024,8]{1,2,0:T(8,128)S(1)} %bitcast.91), channel_id=1, replica_groups=mesh['dp'=2,'tensor'=8,'passage'=16] {'passage'}, dimensions={0}, use_global_device_ids=true | all-gather | bytes 557056 | tf_op jit(solution)/shard_map/all_gather | solution.py:11
  133.7 139.3 %all-gather.6.cloned.1.call-done = f32[16,1024,512]{2,1,0:T(8,128)} async-done(((f32[1,1024,512]{2,1,0:T(8,128)}), f32[16,1024,512]{2,1,0:T(8,128)}) %all-gather.6.cloned.1.call-update) | async-done | bytes 33554448 | tf_op jit(solution)/shard_map/all_gather | solution.py:11
  276.5 139.4 %while.36 = (s32[]{:T(128)}, f32[1024,512]{0,1:T(8,128)}, f32[1024,8]{0,1:T(8,128)S(1)}, f32[1024,8]{0,1:T(8,128)S(1)}, f32[16,1024,8]{1,2,0:T(8,128)}, /*index=...) while((s32[]{:T(128)}, f32[1024,512]{0,1:T(8,128)}, ...), condition=%wide.region_6.7_spmd, body=%wide.region_5.6_spmd.sunk | while | flops 1622021 | bytes 15007895 | solution.py:17
  277.4 3.2 constant_dynamic-slice_fusion.3
  282.5 3.4 fusion.72
  286.7 3.2 constant_dynamic-slice_fusion.3
  291.7 3.4 fusion.72
  295.9 3.2 constant_dynamic-slice_fusion.3
  301.0 3.4 fusion.72
  305.2 3.2 constant_dynamic-slice_fusion.3
  310.3 3.4 fusion.72
  314.5 3.2 constant_dynamic-slice_fusion.3
  319.6 3.4 fusion.72
  328.9 3.4 fusion.72
  333.1 3.2 constant_dynamic-slice_fusion.3
  338.2 3.4 fusion.72
  342.4 3.2 constant_dynamic-slice_fusion.3
  347.5 3.4 fusion.72
  356.8 3.4 fusion.72
  361.0 3.2 constant_dynamic-slice_fusion.3
  366.1 3.4 fusion.72
  375.3 3.4 fusion.72
  379.5 3.2 constant_dynamic-slice_fusion.3
  384.6 3.4 fusion.72
  388.8 3.2 constant_dynamic-slice_fusion.3
  393.9 3.4 fusion.72
  403.2 3.4 fusion.72
  407.4 3.2 constant_dynamic-slice_fusion.3
  412.5 3.4 fusion.72
  417.1 4.1 fusion.49
  421.2 71.1 %all-reduce.2.cloned.1.call-done = f32[64,4096]{1,0:T(8,128)} async-done(((f32[64,4096]{1,0:T(8,128)}), f32[64,4096]{1,0:T(8,128)}) %all-reduce.2.cloned.1.call-update) | async-done | bytes 1048592 | tf_op jit(solution)/shard_map/psum | solution.py:112
  495.1 57.4 %all-gather.8.cloned.1.call-done = bf16[1024,4096]{1,0:T(8,128)(2,1)} async-done(((bf16[64,4096]{1,0:T(8,128)(2,1)}), bf16[1024,4096]{1,0:T(8,128)(2,1)}) %all-gather.8.cloned.1.call-update) | async-done | bytes 8388624 | tf_op jit(solution)/shard_map/all_gather | solution.py:116
  552.5 6.0 fusion.50
  558.6 14.4 %fusion.21 = f32[1024,4096]{1,0:T(8,128)} fusion(bf16[80,4096]{1,0:T(8,128)(2,1)S(1)} %copy-done, bf16[1024,4096]{1,0:T(8,128)(2,1)} %all-gather.8.cloned.1.call-done, bf16[4096,80]{0,1:T(8,128)(2,1)} %param.32, f32[1024,80]{0,1:T(8,128)S(1)} %fusion.50), kind=kOutput, calls=%fused_computation.39 | convolution fusion | flops 1342996480 | bytes 26804224 | tf_op jit(solution)/shard_map/dot_general | solution.py:121
  573.1 183.9 %reduce-scatter.3.cloned.1.call-done = f32[64,4096]{1,0:T(8,128)} async-done(((f32[1024,4096]{1,0:T(8,128)}), f32[64,4096]{1,0:T(8,128)}) %reduce-scatter.3.cloned.1.call-update) | async-done | bytes 1048592 | tf_op jit(solution)/shard_map/reduce_scatter | solution.py:120
  757.1 36.2 %reduce-scatter.5.cloned.1.call-done = f32[64,512]{1,0:T(8,128)} async-done(((f32[64,4096]{1,0:T(8,128)}), f32[64,512]{1,0:T(8,128)}) %reduce-scatter.5.cloned.1.call-update) | async-done | bytes 131088 | tf_op jit(solution)/shard_map/reduce_scatter | solution.py:126
  (106 shorter events, 83.9 us)
Async XLA Ops:
  6.5 552.0 %copy-start = (bf16[80,4096]{1,0:T(8,128)(2,1)S(1)}, bf16[80,4096]{1,0:T(8,128)(2,1)}, u32[]{:S(2)}) copy-start(bf16[80,4096]{1,0:T(8,128)(2,1)} %param.33) | copy-start | bytes 1966084
  6.5 9.3 %copy-start.11 = (s32[1024]{0:T(1024)S(1)}, s32[1024]{0:T(1024)}, u32[]{:S(2)}) copy-start(s32[1024]{0:T(1024)} %constant.243) | copy-start | bytes 12292
  6.5 9.2 %copy-start.13 = (s32[4]{0:T(128)S(1)}, s32[4]{0:T(128)}, u32[]{:S(2)}) copy-start(s32[4]{0:T(128)} %param.25) | copy-start | bytes 52
  6.5 9.2 %copy-start.12 = (f32[32,8]{0,1:T(8,128)S(1)}, f32[32,8]{0,1:T(8,128)}, u32[]{:S(2)}) copy-start(f32[32,8]{0,1:T(8,128)} %param.26) | copy-start | bytes 3076
  6.5 12.3 %copy-start.10 = (s32[4]{0:T(128)S(1)}, s32[4]{0:T(128)}, u32[]{:S(2)}) copy-start(s32[4]{0:T(128)} %param.24) | copy-start | bytes 52
  6.5 44.6 %all-gather.4.cloned.1.call-start = ((), (), s32[]{:S(2)}) async-start(), calls=%async_computation.2 | async-start | bytes 1114112 | tf_op jit(solution)/shard_map/all_gather | solution.py:66
  11.8 46.5 %copy-start.6 = (pred[1024]{0:T(1024)(128)(4,1)S(1)}, pred[1024]{0:T(1024)(128)(4,1)}, u32[]{:S(2)}) copy-start(pred[1024]{0:T(1024)(128)(4,1)} %constant.306) | copy-start | bytes 3076
  11.8 46.5 %copy-start.7 = (pred[1024]{0:T(1024)(128)(4,1)S(1)}, pred[1024]{0:T(1024)(128)(4,1)}, u32[]{:S(2)}) copy-start(pred[1024]{0:T(1024)(128)(4,1)} %constant.307) | copy-start | bytes 3076
  11.8 46.5 %copy-start.8 = (pred[1024]{0:T(1024)(128)(4,1)S(1)}, pred[1024]{0:T(1024)(128)(4,1)}, u32[]{:S(2)}) copy-start(pred[1024]{0:T(1024)(128)(4,1)} %constant.308) | copy-start | bytes 3076
  11.8 261.1 %all-gather.6.cloned.1.call-start = ((), (), s32[]{:S(2)}) async-start(), calls=%async_computation.3 | async-start | bytes 35651584 | tf_op jit(solution)/shard_map/all_gather | solution.py:11
  64.5 4.0 copy-start.2
  82.0 4.0 copy-start.2
  93.5 398.9 %all-reduce.2.cloned.1.call-start = ((), (), s32[]{:S(2)}) async-start(), calls=%async_computation.4 | async-start | bytes 2097152 | tf_op jit(solution)/shard_map/psum | solution.py:112
  113.1 0.8 copy-start.3
  132.9 0.8 copy-start.4
  276.5 215.9 %copy-start.1 = (bf16[64,4096]{1,0:T(8,128)(2,1)S(1)}, bf16[64,4096]{1,0:T(8,128)(2,1)}, u32[]{:S(2)}) copy-start(bf16[64,4096]{1,0:T(8,128)(2,1)} %param.21) | copy-start | bytes 1572868
  415.9 78.0 %copy-start.9 = (f32[4096]{0:T(1024)S(1)}, f32[4096]{0:T(1024)}, u32[]{:S(2)}) copy-start(f32[4096]{0:T(1024)} %param.30) | copy-start | bytes 49156
  415.9 136.6 %copy-start.5 = (bf16[4096,80]{0,1:T(8,128)(2,1)S(1)}, bf16[4096,80]{0,1:T(8,128)(2,1)}, u32[]{:S(2)}) copy-start(bf16[4096,80]{0,1:T(8,128)(2,1)} %param.31) | copy-start | bytes 1966084
  421.2 131.3 %all-gather.8.cloned.1.call-start = ((), (), s32[]{:S(2)}) async-start(), calls=%async_computation.5 | async-start | bytes 8912896 | tf_op jit(solution)/shard_map/all_gather | solution.py:116
  494.9 262.2 %reduce-scatter.3.cloned.1.call-start = ((), (), s32[]{:S(2)}) async-start(), calls=%async_computation.6 | async-start | bytes 17825792 | tf_op jit(solution)/shard_map/reduce_scatter | solution.py:120
  573.1 220.2 %reduce-scatter.5.cloned.1.call-start = ((), (), s32[]{:S(2)}) async-start(), calls=%async_computation.7 | async-start | bytes 1179648 | tf_op jit(solution)/shard_map/reduce_scatter | solution.py:126
Sparse Core Ops, SparseCore 0:
  12.0 39.1 all-gather.3
  93.6 179.2 all-gather.5
  421.3 71.0 all-reduce.1
  495.0 57.4 all-gather.7
  573.2 183.8 reduce-scatter.2
  759.4 33.7 reduce-scatter.4
where the time goes:
time: 809 us; the launch traced here: 802 us
  waiting for transfers between devices  520 us (64%)
  local copies, waits for them, and re-layouts  102 us (13%)
  other arithmetic  82.5 us (10%)
  matrix products  45.2 us (6%)
  blocking collectives  38.5 us (5%)
  between operations  13.6 us (2%)
    reduce_scatter x1, waiting for transfers between devices, on_device(): lax.psum_scatter(jnp.dot(hidden_units, down_weight, preferred_element_typ...  184 us
    all_gather x1, waiting for transfers between devices, joined_2(): everything = jax.tree.map(lambda part: lax.all_gather(part, axis), array)  139 us
    dynamic_slice x30, local copies, waits for them, and re-layouts, turn(): return combine(so_far, jax.tree.map(lambda part: part[k], everything))  76.3 us
    psum x1, waiting for transfers between devices, on_device(): middle = states + lax.psum(projected, 'tensor')  71.1 us
    all_gather x1, waiting for transfers between devices, on_device(): piece = lax.all_gather(ffn_in, 'passage', axis=0, tiled=True)  57.4 us
    add x15, other arithmetic, joined(): out_first.reshape(rows, head_count, -1) * scale_first[..., None]  50.7 us
    all_gather x2, blocking collectives, joined_2(): everything = jax.tree.map(lambda part: lax.all_gather(part, axis), array)  38.5 us
    reduce_scatter x1, waiting for transfers between devices, on_device(): lax.psum_scatter(row_sums, 'tensor', scatter_dimension=1, tiled=True)  36.2 us
  transfers between devices with their start and end apart: 6, of which 6 were waited for; matrix products, arithmetic and copies ran while one was open for 1% of the time, Pallas kernels for 0%

commit v1 on v0

v1 whole, which is shorter than its diff:
```python
import functools

import jax
import jax.numpy as jnp
from jax import lax
from jax.experimental import pallas as pl
from jax.experimental.pallas import tpu as pltpu
from jax.sharding import PartitionSpec as P

PLEN = 256
EPS = 1e-06
BF = jnp.bfloat16
F32 = jnp.float32
MESH = pl.DeviceIdType.MESH
NT = (((1,), (1,)), ((), ()))


def remote(src, dst, send_sem, recv_sem, **where):
    return pltpu.make_async_remote_copy(
        src_ref=src,
        dst_ref=dst,
        send_sem=send_sem,
        recv_sem=recv_sem,
        device_id=where,
        device_id_type=MESH,
    )


def iota(shape, axis):
    return lax.broadcasted_iota(jnp.int32, shape, axis)


def block_kernel(
    states_h, keys_h, values_h, lens_s, srcs_s, bias_s, wq_h, wo_h, again, fgain, gate_h, up_h, down_h,
    out_ref,
    states, wq, wo, kaug, vaug, qaug, sel, expand,
    qall, ostage, srecv, rsend, rrecv,
    wsend, wrecv, wown, mid, midr, fbuf, acc, oown, osend, orecv, fown, fsend, frecv, wall,
    load_sem, wq_sem, ws, wr, qs, qr, qfs, qfr, ss, sr, rs, rr, as_, ar, ms, mr,
    zs, zr, xs, xr, os_, or_, fs, fr,
):
    dp = lax.axis_index("dp")
    z = lax.axis_index("tensor")
    p = lax.axis_index("passage")
    x = p // 4
    yl = (p // 2) % 2
    c = p % 2
    chip = p // 2
    sib = p + 1 - 2 * c
    zpar = z % 2
    zcol = z // 2
    zmate = z + 1 - 2 * zpar

    def peer(dx, dy):
        return ((x + dx) % 4) * 4 + ((yl + dy) % 2) * 2 + c

    def offsets(i):
        d = i // 2
        return d + d // 2 - 2 * (d // 3), i % 2

    def taker(i):
        dx, dy = offsets(i)
        return peer(dx, dy)

    def giver(i):
        dx, dy = offsets(i)
        return peer(4 - dx, 2 - dy)

    ydev = dict(dp=(dp + c) % 2, passage=peer(0, 1))
    zdev = dict(tensor=(z + 1 - 2 * c + 8) % 8)

    barrier = pltpu.get_barrier_semaphore()
    for i in range(1, 8):
        pl.semaphore_signal(barrier, inc=1, device_id={"passage": taker(i)}, device_id_type=MESH)
        pl.semaphore_signal(barrier, inc=1, device_id={"tensor": (z + i) % 8}, device_id_type=MESH)
    pl.semaphore_signal(barrier, inc=1, device_id={"passage": sib}, device_id_type=MESH)
    pl.semaphore_signal(barrier, inc=1, device_id=ydev, device_id_type=MESH)

    loads = [pltpu.make_async_copy(states_h, states, load_sem.at[0])]
    loads[0].start()
    wq_loads = []
    for k in range(4):
        rows = pl.ds(1024 * k, 1024)
        wq_loads.append(pltpu.make_async_copy(wq_h.at[rows], wq.at[rows], wq_sem.at[k]))
        wq_loads[k].start()
    kv_loads = []
    for j in range(4):
        lanes = pl.ds(128 * j, 128)
        kv_loads.append(pltpu.make_async_copy(keys_h.at[:, lanes], kaug.at[j, :, pl.ds(0, 128)], load_sem.at[2 + j]))
        kv_loads.append(pltpu.make_async_copy(values_h.at[:, lanes], vaug.at[j, :, pl.ds(0, 128)], load_sem.at[6 + j]))
    for copy in kv_loads:
        copy.start()
    wo_load = pltpu.make_async_copy(wo_h, wo, load_sem.at[1])
    wo_load.start()
    own_loads = []
    for m, ref in enumerate((gate_h, up_h, down_h)):
        own_loads.append(pltpu.make_async_copy(ref, wall.at[m, 0], load_sem.at[10 + m]))
        own_loads[m].start()

    loads[0].wait()
    square = jnp.zeros((64, 1), F32)
    for k in range(4):
        part = states[:, 1024 * k : 1024 * (k + 1)].astype(F32)
        square = square + jnp.sum(part * part, axis=-1, keepdims=True)
    scale = lax.rsqrt(square * (1.0 / 4096) + EPS)
    query = jnp.zeros((64, 512), F32)
    for k in range(4):
        cols = slice(1024 * k, 1024 * (k + 1))
        normed = (states[:, cols].astype(F32) * scale * again[:, cols]).astype(BF)
        wq_loads[k].wait()
        query = query + jnp.dot(normed, wq[cols, :], preferred_element_type=F32)
    qall[p] = query.astype(BF)

    pl.semaphore_wait(barrier, 16)

    def q_send(i):
        return remote(qall.at[p], qall.at[p], qs.at[i], qr.at[i], passage=taker(i))

    def q_arrival(i):
        slot = qall.at[giver(i)]
        return remote(slot, slot, qs.at[i], qr.at[i], passage=taker(i))

    def q_hand(i):
        slot = qall.at[giver(i)]
        return remote(slot, slot, qfs.at[i], qfr.at[i], passage=sib)

    def q_handed(i):
        dx, dy = offsets(i)
        slot = qall.at[((x + 4 - dx) % 4) * 4 + ((yl + 2 - dy) % 2) * 2 + 1 - c]
        return remote(slot, slot, qfs.at[i], qfr.at[i], passage=sib)

    q_hand(0).start()
    for i in range(1, 8):
        q_send(i).start()

    def w_copy(kind, m):
        own = (gate_h, up_h, down_h)[m]
        if kind == 0:
            src, slot, dev = own, 1, ydev
        elif kind == 1:
            src, slot, dev = own, 2, zdev
        elif kind == 2:
            src, slot, dev = own, 4, dict(passage=sib)
        elif kind < 6:
            src, slot, dev = wall.at[m, kind - 2], kind + 2, dict(passage=sib)
        else:
            src, slot, dev = wall.at[m, 2], 3, ydev
        return remote(src, wall.at[m, slot], ws.at[kind, m], wr.at[kind, m], **dev)

    for m in range(3):
        for kind in range(3):
            w_copy(kind, m).start()

    lane = iota((256, 128), 1)
    row = iota((256, 128), 0)
    for j in range(4):
        for pp in range(4):
            table = jnp.where(lane == 0, jnp.where(row >= lens_s[pp], F32(-1e30), F32(0)), F32(0))
            for e in range(2):
                value = jnp.full((256, 128), bias_s[2 * j + e, srcs_s[pp]], F32)
                high = value.astype(BF).astype(F32)
                middle = (value - high).astype(BF).astype(F32)
                low = value - high - middle
                first = 1 + 3 * e
                table = jnp.where(lane == first, high, table)
                table = jnp.where(lane == first + 1, middle, table)
                table = jnp.where(lane == first + 2, low, table)
            kaug[j, 256 * pp : 256 * (pp + 1), 128:256] = table.astype(BF)
        vaug[j, :, 128:256] = jnp.ones((1024, 128), BF)
    upper = row < 128
    qaug[...] = jnp.where(
        (lane == 0) | (upper & (lane >= 1) & (lane < 4)) | (~upper & (lane >= 4) & (lane < 7)), F32(1), F32(0)
    ).astype(BF)
    srow, scol = iota((1536, 128), 0), iota((1536, 128), 1)
    sel[...] = jnp.where((srow % 64 == 0) & (scol == srow // 64), F32(1), F32(0)).astype(BF)
    erow, ecol = iota((128, 512), 0), iota((128, 512), 1)
    expand[...] = jnp.where((erow < 24) & (erow % 8 == ecol // 64), F32(1), F32(0)).astype(BF)
    for copy in kv_loads:
        copy.wait()

    def attend(i):
        dx, dy = offsets(i)
        source = ((x + 4 - dx) % 4) * 2 + (yl + 2 - dy) % 2
        rows = qall[pl.ds(2 * source, 2)].reshape(128, 512)
        head_lane = iota((128, 128), 1) < 64
        zero = jnp.zeros((128, 128), BF)
        for j in range(4):
            cols = slice(128 * j, 128 * (j + 1))
            pair = rows[:, cols]
            both = jnp.concatenate([jnp.where(head_lane, pair, zero), jnp.where(head_lane, zero, pair)], axis=0)
            both = jnp.concatenate([both, qaug[...]], axis=1)
            scores = lax.dot_general(both, kaug[j], NT, preferred_element_type=F32)
            peak = jnp.max(scores, axis=1, keepdims=True)
            weights = jnp.exp(scores - peak).astype(BF)
            result = jnp.dot(weights, vaug[j], preferred_element_type=F32)
            total = result[:, 128:]
            part = result[:, :128] / total
            level = peak + jnp.log(total)
            part = jnp.where(head_lane, part[:128], part[128:])
            level = jnp.where(head_lane, level[:128], level[128:])
            ostage[i, 0, 0, :, cols] = part[:64]
            ostage[i, 1, 0, :, cols] = part[64:]
            ostage[i, 0, 1, :, cols] = level[:64]
            ostage[i, 1, 1, :, cols] = level[64:]

    def half_send(i):
        return remote(ostage.at[i, 1 - c], srecv.at[i], ss.at[i], sr.at[i], passage=sib)

    def part_send(i):
        return remote(rsend.at[i], rrecv.at[i], rs.at[i], rr.at[i], passage=giver(i))

    def merge(i):
        half_send(i).wait_recv()
        part_a, level_a = ostage[i, c, 0], ostage[i, c, 1]
        part_b, level_b = srecv[i, 0], srecv[i, 1]
        highest = jnp.maximum(level_a, level_b)
        weight_a = jnp.exp(level_a - highest)
        weight_b = jnp.exp(level_b - highest)
        total = weight_a + weight_b
        rsend[i, :, 0:512] = ((weight_a * part_a + weight_b * part_b) / total).astype(BF)
        level = highest + jnp.log(total)
        high = level.astype(BF)
        rest = level - high.astype(F32)
        middle = rest.astype(BF)
        low = (rest - middle.astype(F32)).astype(BF)
        pieces = jnp.concatenate([high, middle, low], axis=1)
        rsend[i, :, 512:640] = jnp.dot(pieces, sel[...], preferred_element_type=F32).astype(BF)

    def turn(i, carry):
        @pl.when(i < 7)
        def _():
            q_arrival(i + 1).wait_recv()
            q_hand(i + 1).start()

        q_handed(i).wait_recv()
        attend(i)
        half_send(i).start()

        @pl.when(i >= 1)
        def _():
            merge(i - 1)

        @pl.when(i >= 2)
        def _():
            part_send(i - 1).start()

        return carry

    lax.fori_loop(0, 8, turn, 0)
    merge(7)
    part_send(7).start()

    for m in range(3):
        w_copy(1, m).wait_recv()
        w_copy(6, m).start()
        w_copy(4, m).start()
    for m in range(3):
        w_copy(0, m).wait_recv()
        w_copy(3, m).start()

    for i in range(1, 8):
        part_send(i).wait_recv()
    levels = [
        jnp.dot((rsend[0] if i == 0 else rrecv[i])[:, 512:640], expand[...], preferred_element_type=F32)
        for i in range(8)
    ]
    highest = functools.reduce(jnp.maximum, levels)
    total = jnp.zeros((64, 512), F32)
    joined = jnp.zeros((64, 512), F32)
    for i in range(8):
        weight = jnp.exp(levels[i] - highest)
        total = total + weight
        joined = joined + weight * (rsend[0] if i == 0 else rrecv[i])[:, 0:512].astype(F32)
    attended = (joined / total).astype(BF)

    wo_load.wait()

    def wo_send(o):
        to = (z + o) % 8
        return remote(wsend.at[to // 2, to % 2], wrecv.at[o], as_.at[o], ar.at[o], tensor=to)

    for k in (2, 1, 3, 0):
        block = (zcol + k) % 4
        lanes = pl.ds(pl.multiple_of(block * 1024, 1024), 1024)
        product = jnp.dot(attended, wo[:, lanes], preferred_element_type=F32)
        wsend[block, 0] = product[:32].astype(BF)
        wsend[block, 1] = product[32:].astype(BF)
        if k == 0:
            wown[0] = product[:32]
            wown[1] = product[32:]
            wo_send((zmate - z + 8) % 8).start()
        else:
            for e in range(2):
                wo_send((2 * block + e - z + 8) % 8).start()

    lanes = pl.ds(pl.multiple_of(zcol * 1024, 1024), 1024)
    middle = states[pl.ds(pl.multiple_of(zpar * 32, 32), 32), lanes].astype(F32) + wown[zpar]
    for o in range(1, 8):
        wo_send(o).wait_recv()
        middle = middle + wrecv[o].astype(F32)
    mid[0] = middle[:, :512]
    mid[1] = middle[:, 512:]
    fbuf[zcol, x] = (middle * fgain[:, lanes]).astype(BF)

    def z_send(o):
        slot = fbuf.at[zcol, x]
        return remote(slot, slot, zs.at[o], zr.at[o], tensor=(z + 2 * o) % 8)

    def z_arrival(o):
        slot = fbuf.at[((z + 8 - 2 * o) % 8) // 2, x]
        return remote(slot, slot, zs.at[o], zr.at[o], tensor=(z + 2 * o) % 8)

    def x_send(o, d):
        slot = fbuf.at[((z + 8 - 2 * o) % 8) // 2, x]
        return remote(slot, slot, xs.at[o, d], xr.at[o, d], passage=peer(d, 0))

    def x_arrival(o, d):
        slot = fbuf.at[((z + 8 - 2 * o) % 8) // 2, (x + 4 - d) % 4]
        return remote(slot, slot, xs.at[o, d], xr.at[o, d], passage=peer(d, 0))

    for o in (1, 3, 2):
        z_send(o).start()
    for d in (1, 3, 2):
        x_send(0, d).start()
    mid_send = remote(mid.at[1 - zpar], midr, ms, mr, tensor=zmate)
    mid_send.start()

    for m in range(3):
        w_copy(6, m).wait_recv()
        w_copy(5, m).start()
    for copy in own_loads:
        copy.wait()
    for kind in (2, 3, 4, 5):
        for m in range(2):
            w_copy(kind, m).wait_recv()

    squares = jnp.zeros((128, 1), F32)
    order = (0, 1, 3, 2)
    for n, o in enumerate(order):
        if n < 3:
            z_arrival(order[n + 1]).wait_recv()
            for d in (1, 3, 2):
                x_send(order[n + 1], d).start()
        for d in (1, 3, 2):
            x_arrival(o, d).wait_recv()
        block = ((z + 8 - 2 * o) % 8) // 2
        lanes = pl.ds(pl.multiple_of(block * 1024, 1024), 1024)
        piece = fbuf[block].reshape(128, 1024)
        plain = piece.astype(F32) / fgain[:, lanes]
        squares = squares + jnp.sum(plain * plain, axis=-1, keepdims=True)
        for m in range(2):
            weight = wall[m, :, :, lanes].reshape(640, 1024)
            product = lax.dot_general(piece, weight, NT, preferred_element_type=F32)
            if n == 0:
                acc[m] = product
            else:
                acc[m] += product
    scale = lax.rsqrt(squares * (1.0 / 4096) + EPS)
    gate = acc[0] * scale
    hidden = (jax.nn.gelu(gate, approximate=True) * (acc[1] * scale)).astype(BF)

    for kind in (2, 3, 4, 5):
        w_copy(kind, 2).wait_recv()

    def o_send(block, k, d):
        return remote(osend.at[block, (x + d) % 4], orecv.at[k, d], os_.at[k, d], or_.at[k, d], passage=peer(d, 0))

    for k in (2, 1, 3, 0):
        block = (zcol + k) % 4
        lanes = pl.ds(pl.multiple_of(block * 1024, 1024), 1024)
        product = jnp.dot(hidden, wall[2, :, :, lanes].reshape(640, 1024), preferred_element_type=F32)
        product = product.reshape(4, 32, 1024)
        osend[block] = product.astype(BF)
        oown[k] = product
        for d in (1, 3, 2):
            o_send(block, k, d).start()

    def f_send(o):
        to = (z + o) % 8
        return remote(fsend.at[to // 2, to % 2], frecv.at[o], fs.at[o], fr.at[o], tensor=to)

    for k in (2, 1, 3, 0):
        block = (zcol + k) % 4
        total = oown[k, x]
        for d in (1, 3, 2):
            o_send(block, k, d).wait_recv()
            total = total + orecv[k, d].astype(F32)
        fsend[block, 0] = total[:, :512].astype(BF)
        fsend[block, 1] = total[:, 512:].astype(BF)
        if k == 0:
            fown[0] = total[:, :512]
            fown[1] = total[:, 512:]
            f_send((zmate - z + 8) % 8).start()
        else:
            for e in range(2):
                f_send((2 * block + e - z + 8) % 8).start()

    mid_send.wait_recv()
    mine = mid[zpar] + fown[zpar]
    other = midr[...]
    for o in range(1, 8):
        f_send(o).wait_recv()
        if o % 2 == 0:
            mine = mine + frecv[o].astype(F32)
        else:
            other = other + frecv[o].astype(F32)
    out_ref[pl.ds(pl.multiple_of(zpar * 32, 32), 32), :] = mine.astype(BF)
    out_ref[pl.ds(pl.multiple_of(32 - zpar * 32, 32), 32), :] = other.astype(BF)

    for i in range(8):
        q_hand(i).wait_send()
        half_send(i).wait_send()
        if i > 0:
            q_send(i).wait_send()
            part_send(i).wait_send()
            wo_send(i).wait_send()
            f_send(i).wait_send()
    for m in range(3):
        for kind in range(7):
            w_copy(kind, m).wait_send()
    mid_send.wait_send()
    for o in range(4):
        if o > 0:
            z_send(o).wait_send()
        for d in (1, 2, 3):
            x_send(o, d).wait_send()
            o_send((zcol + o) % 4, o, d).wait_send()


def on_device(
    answer_states, cross_keys, cross_values, passage_lengths, passage_sources, source_bias,
    query_weight, output_weight, attn_gain, ffn_gain, gate_weight, up_weight, down_weight,
):
    hbm = pl.BlockSpec(memory_space=pl.ANY)
    smem = pl.BlockSpec(memory_space=pltpu.SMEM)
    vmem = pl.BlockSpec(memory_space=pltpu.VMEM)
    dma = pltpu.SemaphoreType.DMA
    return pl.pallas_call(
        block_kernel,
        out_shape=jax.ShapeDtypeStruct((64, 512), BF),
        in_specs=[hbm, hbm, hbm, smem, smem, smem, hbm, hbm, vmem, vmem, hbm, hbm, hbm],
        out_specs=vmem,
        scratch_shapes=[
            pltpu.VMEM((64, 4096), BF),
            pltpu.VMEM((4096, 512), BF),
            pltpu.VMEM((512, 4096), BF),
            pltpu.VMEM((4, 1024, 256), BF),
            pltpu.VMEM((4, 1024, 256), BF),
            pltpu.VMEM((256, 128), BF),
            pltpu.VMEM((1536, 128), BF),
            pltpu.VMEM((128, 512), BF),
            pltpu.VMEM((16, 64, 512), BF),
            pltpu.VMEM((8, 2, 2, 64, 512), F32),
            pltpu.VMEM((8, 2, 64, 512), F32),
            pltpu.VMEM((8, 64, 640), BF),
            pltpu.VMEM((8, 64, 640), BF),
            pltpu.VMEM((4, 2, 32, 1024), BF),
            pltpu.VMEM((8, 32, 1024), BF),
            pltpu.VMEM((2, 32, 1024), F32),
            pltpu.VMEM((2, 32, 512), F32),
            pltpu.VMEM((32, 512), F32),
            pltpu.VMEM((4, 4, 32, 1024), BF),
            pltpu.VMEM((2, 128, 640), F32),
            pltpu.VMEM((4, 4, 32, 1024), F32),
            pltpu.VMEM((4, 4, 32, 1024), BF),
            pltpu.VMEM((4, 4, 32, 1024), BF),
            pltpu.VMEM((2, 32, 512), F32),
            pltpu.VMEM((4, 2, 32, 512), BF),
            pltpu.VMEM((8, 32, 512), BF),
            pltpu.VMEM((3, 8, 80, 4096), BF),
            dma((13,)), dma((4,)),
            dma((7, 3)), dma((7, 3)),
            dma((8,)), dma((8,)), dma((8,)), dma((8,)),
            dma((8,)), dma((8,)), dma((8,)), dma((8,)),
            dma((8,)), dma((8,)), dma, dma,
            dma((4,)), dma((4,)), dma((4, 4)), dma((4, 4)),
            dma((4, 4)), dma((4, 4)), dma((8,)), dma((8,)),
        ],
        compiler_params=pltpu.CompilerParams(
            collective_id=0, has_side_effects=True, vmem_limit_bytes=60 * 1024 * 1024
        ),
        cost_estimate=pl.CostEstimate(flops=5_000_000_000, bytes_accessed=14_000_000, transcendentals=9_000_000),
        name="decoder_block",
    )(
        answer_states, cross_keys, cross_values, passage_lengths, passage_sources, source_bias.T,
        query_weight, output_weight, attn_gain.reshape(1, 4096), ffn_gain.reshape(1, 4096),
        gate_weight.T, up_weight.T, down_weight,
    )


def solution(mesh):
    return jax.shard_map(
        on_device,
        mesh=mesh,
        in_specs=(
            P(("dp", "passage"), None),
            P(("dp", "passage"), "tensor"),
            P(("dp", "passage"), "tensor"),
            P(("dp", "passage")),
            P(("dp", "passage")),
            P(None, "tensor"),
            P(None, "tensor"),
            P("tensor", None),
            P(),
            P(),
            P(None, ("tensor", "passage")),
            P(None, ("tensor", "passage")),
            P(("tensor", "passage"), None),
        ),
        out_specs=P(("dp", "passage"), "tensor"),
        check_vma=False,
    )
```

time: 809 us -> 96.5 us (0.12)
  the two profiles are of different devices: /device:TPU:1 before, /device:TPU:16 now
where the time goes in v1:
time: 96.5 us; the launch traced here: 96.4 us
  Pallas kernels  94.9 us (98%)
  local copies, waits for them, and re-layouts  1.47 us (2%)
    pallas_call x1, Pallas kernels, on_device(): pl.pallas_call(block_kernel, out_shape=jax.ShapeDtypeStruct((64, 512), BF...  94.9 us

profile of v1, /device:TPU:16, one launch (start us, length us, event | category | flops | bytes accessed | tf_op | source)
XLA Modules:
  0.0 96.4 jit_solution(12638361487970657578)
XLA Ops:
  0.0 94.9 %decoder_block.1 = bf16[64,512]{1,0:T(8,128)(2,1)} custom-call(bf16[64,4096]{1,0:T(8,128)(2,1)} %states_h.1, bf16[1024,512]{1,0:T(8,128)(2,1)} %keys_h.1, bf16[1024,512]{1,0:T(8,128)(2,1)} %values_h.1, s32[4]{0:T(128)} %lens_s.1, s32[4]{0:T(128)} %srcs_s.1, f32[8,32]{1,0:T(8,128)} %bitcast.9, bf16[4096,512]{1,0:T(8,128)(2,1)} %wq_h.1, ...), custom_call_target="tpu_custom_call" | custom-call | flops 5000000000 | bytes 14000000 | tf_op jit(solution)/shard_map/decoder_block/pallas_call | solution.py:438
  94.9 1.5 %copy.15 = bf16[64,512]{1,0:T(8,128)(2,1)} copy(bf16[64,512]{1,0:T(8,128)(2,1)} %decoder_block.1) | data formatting | bytes 131072

commit v2 on v1

v2 whole, which is shorter than its diff:
```python
import functools

import jax
import jax.numpy as jnp
from jax import lax
from jax.experimental import pallas as pl
from jax.experimental.pallas import tpu as pltpu
from jax.sharding import PartitionSpec as P

PLEN = 256
EPS = 1e-06
BF = jnp.bfloat16
F32 = jnp.float32
MESH = pl.DeviceIdType.MESH
NT = (((1,), (1,)), ((), ()))


def remote(src, dst, send_sem, recv_sem, **where):
    return pltpu.make_async_remote_copy(
        src_ref=src,
        dst_ref=dst,
        send_sem=send_sem,
        recv_sem=recv_sem,
        device_id=where,
        device_id_type=MESH,
    )


def iota(shape, axis):
    return lax.broadcasted_iota(jnp.int32, shape, axis)


def block_kernel(
    states_h, keys_h, values_h, lens_s, srcs_s, bias_s, wq_h, wo_h, again, fgain, gate_h, up_h, down_h,
    out_ref,
    states, wq, wo, kaug, vaug, qaug, sel, expand,
    qall, ostage, srecv, rsend, rrecv,
    wsend, wrecv, wown, mid, midr, fbuf, acc, oown, osend, orecv, fown, fsend, frecv, wall,
    load_sem, wq_sem, ws, wr, qs, qr, qfs, qfr, ss, sr, rs, rr, as_, ar, ms, mr,
    zs, zr, xs, xr, os_, or_, fs, fr,
):
    dp = lax.axis_index("dp")
    z = lax.axis_index("tensor")
    p = lax.axis_index("passage")
    x = p // 4
    yl = (p // 2) % 2
    c = p % 2
    sib = p + 1 - 2 * c
    zpar = z % 2
    zcol = z // 2
    zmate = z + 1 - 2 * zpar

    def peer(dx, dy):
        return ((x + dx) % 4) * 4 + ((yl + dy) % 2) * 2 + c

    def shift(t):
        return t + t // 2 - 2 * (t // 3)

    ydev = dict(dp=(dp + c) % 2, passage=peer(0, 1))
    yfar = dict(dp=1 - dp, passage=peer(0, 1))
    zdev = dict(tensor=(z + 1 - 2 * c + 8) % 8)

    barrier = pltpu.get_barrier_semaphore()
    for i in range(1, 8):
        pl.semaphore_signal(barrier, inc=1, device_id={"passage": peer(i // 2, i % 2)}, device_id_type=MESH)
        pl.semaphore_signal(barrier, inc=1, device_id={"tensor": (z + i) % 8}, device_id_type=MESH)
    pl.semaphore_signal(barrier, inc=1, device_id={"passage": sib}, device_id_type=MESH)
    pl.semaphore_signal(barrier, inc=1, device_id=yfar, device_id_type=MESH)

    states_load = pltpu.make_async_copy(states_h, states, load_sem.at[0])
    states_load.start()
    wq_loads = []
    for k in range(4):
        rows = pl.ds(1024 * k, 1024)
        wq_loads.append(pltpu.make_async_copy(wq_h.at[rows], wq.at[rows], wq_sem.at[k]))
        wq_loads[k].start()
    kv_loads = []
    for j in range(4):
        lanes = pl.ds(128 * j, 128)
        kv_loads.append(pltpu.make_async_copy(keys_h.at[:, lanes], kaug.at[j, :, pl.ds(0, 128)], load_sem.at[2 + j]))
        kv_loads.append(pltpu.make_async_copy(values_h.at[:, lanes], vaug.at[j, :, pl.ds(0, 128)], load_sem.at[6 + j]))
    wo_load = pltpu.make_async_copy(wo_h, wo, load_sem.at[1])
    own_loads = [
        pltpu.make_async_copy(ref, wall.at[m, 0], load_sem.at[10 + m]) for m, ref in enumerate((gate_h, up_h, down_h))
    ]

    states_load.wait()
    square = jnp.zeros((64, 1), F32)
    for k in range(4):
        part = states[:, 1024 * k : 1024 * (k + 1)].astype(F32)
        square = square + jnp.sum(part * part, axis=-1, keepdims=True)
    scale = lax.rsqrt(square * (1.0 / 4096) + EPS)
    query = jnp.zeros((64, 512), F32)
    for k in range(4):
        cols = slice(1024 * k, 1024 * (k + 1))
        normed = (states[:, cols].astype(F32) * scale * again[:, cols]).astype(BF)
        wq_loads[k].wait()
        query = query + jnp.dot(normed, wq[cols, :], preferred_element_type=F32)
    for copy in kv_loads:
        copy.start()
    qall[0, x, c, yl] = query[:32].astype(BF)
    qall[1, x, c, yl] = query[32:].astype(BF)

    pl.semaphore_wait(barrier, 16)

    def q_send(b, t, dy):
        slot = qall.at[b, x, c, yl]
        return remote(slot, slot, qs.at[b, t, dy], qr.at[b, t, dy], passage=peer(shift(t), dy))

    def q_arrival(b, t, dy):
        slot = qall.at[b, (x + 4 - shift(t)) % 4, c, (yl + dy) % 2]
        return remote(slot, slot, qs.at[b, t, dy], qr.at[b, t, dy], passage=peer(shift(t), dy))

    def q_hand(b, t):
        slab = qall.at[b, (x + 4 - shift(t)) % 4, c]
        return remote(slab, slab, qfs.at[b, t], qfr.at[b, t], passage=sib)

    def q_handed(b, t):
        slab = qall.at[b, (x + 4 - shift(t)) % 4, 1 - c]
        return remote(slab, slab, qfs.at[b, t], qfr.at[b, t], passage=sib)

    others = [(t, dy) for t in range(4) for dy in range(2) if (t, dy) != (0, 0)]
    for t, dy in others:
        q_send(0, t, dy).start()

    def w_copy(kind, m):
        own = (gate_h, up_h, down_h)[m]
        if kind == 0:
            src, slot, dev = own, 2, yfar if m == 2 else ydev
        elif kind == 1:
            src, slot, dev = own, 4, zdev
        elif kind == 2:
            src, slot, dev = own, 1, dict(passage=sib)
        elif kind < 6:
            src, slot, dev = wall.at[m, 2 * kind - 4], 2 * kind - 3, dict(passage=sib)
        else:
            src, slot, dev = wall.at[m, 4], 6, ydev
        return remote(src, wall.at[m, slot], ws.at[kind, m], wr.at[kind, m], **dev)

    w_copy(0, 0).start()
    for m in range(3):
        w_copy(1, m).start()

    lane = iota((256, 128), 1)
    row = iota((256, 128), 0)
    for j in range(4):
        for pp in range(4):
            table = jnp.where(lane == 0, jnp.where(row >= lens_s[pp], F32(-1e30), F32(0)), F32(0))
            for e in range(2):
                value = jnp.full((256, 128), bias_s[2 * j + e, srcs_s[pp]], F32)
                high = value.astype(BF).astype(F32)
                middle = (value - high).astype(BF).astype(F32)
                low = value - high - middle
                first = 1 + 3 * e
                table = jnp.where(lane == first, high, table)
                table = jnp.where(lane == first + 1, middle, table)
                table = jnp.where(lane == first + 2, low, table)
            kaug[j, 256 * pp : 256 * (pp + 1), 128:256] = table.astype(BF)
        vaug[j, :, 128:256] = jnp.ones((1024, 128), BF)
    upper = row < 128
    qaug[...] = jnp.where(
        (lane == 0) | (upper & (lane >= 1) & (lane < 4)) | (~upper & (lane >= 4) & (lane < 7)), F32(1), F32(0)
    ).astype(BF)
    srow, scol = iota((1536, 128), 0), iota((1536, 128), 1)
    sel[...] = jnp.where((srow % 64 == 0) & (scol == srow // 64), F32(1), F32(0)).astype(BF)
    erow, ecol = iota((128, 512), 0), iota((128, 512), 1)
    expand[...] = jnp.where((erow < 24) & (erow % 8 == ecol // 64), F32(1), F32(0)).astype(BF)
    q_arrival(0, 0, 1).wait_recv()
    q_hand(0, 0).start()
    for copy in kv_loads:
        copy.wait()
    wo_load.start()
    for copy in own_loads:
        copy.start()
    for m in range(3):
        w_copy(2, m).start()

    def attend(n):
        rows = qall[n // 4, (x + 4 - shift(n % 4)) % 4].reshape(128, 512)
        head_lane = iota((128, 128), 1) < 64
        zero = jnp.zeros((128, 128), BF)
        for j in range(4):
            cols = slice(128 * j, 128 * (j + 1))
            pair = rows[:, cols]
            both = jnp.concatenate([jnp.where(head_lane, pair, zero), jnp.where(head_lane, zero, pair)], axis=0)
            both = jnp.concatenate([both, qaug[...]], axis=1)
            scores = lax.dot_general(both, kaug[j], NT, preferred_element_type=F32)
            peak = jnp.max(scores, axis=1, keepdims=True)
            weights = jnp.exp(scores - peak).astype(BF)
            result = jnp.dot(weights, vaug[j], preferred_element_type=F32)
            part = jnp.where(head_lane, result[:128, :128], result[128:, :128])
            total = jnp.where(head_lane, result[:128, 128:], result[128:, 128:])
            peak = jnp.where(head_lane, peak[:128], peak[128:])
            for e in range(2):
                half = slice(64 * e, 64 * (e + 1))
                ostage[n, e, 0, :, cols] = part[half]
                ostage[n, e, 1, :, cols] = total[half]
                ostage[n, e, 2, :, cols] = peak[half]

    def half_send(n):
        return remote(ostage.at[n, 1 - c], srecv.at[n], ss.at[n], sr.at[n], passage=sib)

    def part_send(b, t, dy):
        to = ((x + 4 - shift(t)) % 4) * 4 + ((yl + dy) % 2) * 2 + c
        return remote(
            rsend.at[4 * b + t, (yl + dy) % 2], rrecv.at[b, t, dy], rs.at[b, t, dy], rr.at[b, t, dy], passage=to
        )

    def merge(n):
        half_send(n).wait_recv()
        peak_a, peak_b = ostage[n, c, 2], srecv[n, 2]
        highest = jnp.maximum(peak_a, peak_b)
        weight_a = jnp.exp(peak_a - highest)
        weight_b = jnp.exp(peak_b - highest)
        total = weight_a * ostage[n, c, 1] + weight_b * srecv[n, 1]
        part = ((weight_a * ostage[n, c, 0] + weight_b * srecv[n, 0]) / total).astype(BF)
        level = highest + jnp.log(total)
        high = level.astype(BF)
        rest = level - high.astype(F32)
        middle = rest.astype(BF)
        low = (rest - middle.astype(F32)).astype(BF)
        pieces = jnp.concatenate([high, middle, low], axis=1)
        packed = jnp.dot(pieces, sel[...], preferred_element_type=F32).astype(BF)
        for e in range(2):
            rsend[n, e, :, 0:512] = part[32 * e : 32 * (e + 1)]
            rsend[n, e, :, 512:640] = packed[32 * e : 32 * (e + 1)]
        b, t = n // 4, n % 4
        part_send(b, t, 1).start()

        @pl.when(t > 0)
        def _():
            part_send(b, t, 0).start()

    def wo_send(b, o):
        to = (z + o) % 8
        return remote(wsend.at[b, to // 2, to % 2], wrecv.at[b, o], as_.at[b, o], ar.at[b, o], tensor=to)

    def project(b):
        for t, dy in others:
            part_send(b, t, dy).wait_recv()
        parts = [rsend[4 * b, yl]] + [rrecv[b, t, dy] for t, dy in others]
        levels = [jnp.dot(part[:, 512:640], expand[...], preferred_element_type=F32) for part in parts]
        highest = functools.reduce(jnp.maximum, levels)
        total = jnp.zeros((32, 512), F32)
        joined = jnp.zeros((32, 512), F32)
        for part, level in zip(parts, levels):
            weight = jnp.exp(level - highest)
            total = total + weight
            joined = joined + weight * part[:, 0:512].astype(F32)
        attended = (joined / total).astype(BF)
        for k in (2, 1, 3, 0):
            block = (zcol + k) % 4
            lanes = pl.ds(pl.multiple_of(block * 1024, 1024), 1024)
            product = jnp.dot(attended, wo[:, lanes], preferred_element_type=F32)
            wsend[b, block, 0] = product[:16].astype(BF)
            wsend[b, block, 1] = product[16:].astype(BF)
            if k == 0:
                wown[b, 0] = product[:16]
                wown[b, 1] = product[16:]
                wo_send(b, (zmate - z + 8) % 8).start()
            else:
                for e in range(2):
                    wo_send(b, (2 * block + e - z + 8) % 8).start()

    def z_send(b, o):
        slot = fbuf.at[zcol, b, x]
        return remote(slot, slot, zs.at[b, o], zr.at[b, o], tensor=(z + 2 * o) % 8)

    def z_arrival(b, o):
        slot = fbuf.at[((z + 8 - 2 * o) % 8) // 2, b, x]
        return remote(slot, slot, zs.at[b, o], zr.at[b, o], tensor=(z + 2 * o) % 8)

    def x_send(b, o, d):
        slot = fbuf.at[((z + 8 - 2 * o) % 8) // 2, b, x]
        return remote(slot, slot, xs.at[b, o, d], xr.at[b, o, d], passage=peer(d, 0))

    def x_arrival(b, o, d):
        slot = fbuf.at[((z + 8 - 2 * o) % 8) // 2, b, (x + 4 - d) % 4]
        return remote(slot, slot, xs.at[b, o, d], xr.at[b, o, d], passage=peer(d, 0))

    def residual(b):
        lanes = pl.ds(pl.multiple_of(zcol * 1024, 1024), 1024)
        rows = pl.ds(pl.multiple_of(32 * b + zpar * 16, 16), 16)
        middle = states[rows, lanes].astype(F32) + wown[b, zpar]
        for o in range(1, 8):
            wo_send(b, o).wait_recv()
            middle = middle + wrecv[b, o].astype(F32)
        mid[0, 16 * b : 16 * b + 16] = middle[:, :512]
        mid[1, 16 * b : 16 * b + 16] = middle[:, 512:]
        fbuf[zcol, b, x] = (middle * fgain[:, lanes]).astype(BF)
        for o in (1, 3, 2):
            z_send(b, o).start()
        for d in (1, 3, 2):
            x_send(b, 0, d).start()

    def forward(b, o):
        z_arrival(b, o).wait_recv()
        for d in (1, 3, 2):
            x_send(b, o, d).start()

    def turn(n, carry):
        after = n + 1

        @pl.when((n < 7) & (after % 4 > 0))
        def _():
            q_arrival(after // 4, after % 4, 0).wait_recv()

        @pl.when(n < 7)
        def _():
            q_arrival(after // 4, after % 4, 1).wait_recv()
            q_hand(after // 4, after % 4).start()

        q_handed(n // 4, n % 4).wait_recv()
        attend(n)
        half_send(n).start()

        @pl.when(n == 0)
        def _():
            for t, dy in others:
                q_send(1, t, dy).start()

        @pl.when(n >= 1)
        def _():
            merge(n - 1)

        @pl.when(n == 5)
        def _():
            wo_load.wait()
            project(0)

        for m in range(1, 3):

            @pl.when(n == 2 * m - 2)
            def _():
                w_copy(0, m).start()

        for m in range(3):

            @pl.when(n == 4 + m)
            def _():
                w_copy(0, m).wait_recv()
                w_copy(1, m).wait_recv()
                w_copy(6, m).start()
                w_copy(3, m).start()
                w_copy(4, m).start()

        return carry

    lax.fori_loop(0, 8, turn, 0)
    merge(7)
    residual(0)

    project(1)
    for o in (1, 3, 2):
        forward(0, o)
    residual(1)
    mid_send = remote(mid.at[1 - zpar], midr, ms, mr, tensor=zmate)
    mid_send.start()
    for o in (1, 3, 2):
        forward(1, o)

    for copy in own_loads:
        copy.wait()

    def gate_up(block, first, last):
        lanes = pl.ds(pl.multiple_of(block * 1024, 1024), 1024)
        piece = fbuf[block].reshape(128, 1024)
        units = 80 * (last - first)
        return [
            lax.dot_general(piece, wall[m, first:last, :, lanes].reshape(units, 1024), NT, preferred_element_type=F32)
            for m in range(2)
        ]

    def activate(sums, scale):
        gate = sums[0] * scale
        return (jax.nn.gelu(gate, approximate=True) * (sums[1] * scale)).astype(BF)

    for m in range(2):
        for kind in (2, 3, 4):
            w_copy(kind, m).wait_recv()
    squares = jnp.zeros((128, 1), F32)
    for n, o in enumerate((0, 1, 3, 2)):
        for b in range(2):
            for d in (1, 3, 2):
                x_arrival(b, o, d).wait_recv()
        block = ((z + 8 - 2 * o) % 8) // 2
        plain = fbuf[block].reshape(128, 1024).astype(F32) / fgain[:, pl.ds(pl.multiple_of(block * 1024, 1024), 1024)]
        squares = squares + jnp.sum(plain * plain, axis=-1, keepdims=True)
        for m, product in enumerate(gate_up(block, 0, 6)):
            if n == 0:
                acc[m] = product
            else:
                acc[m] += product
    scale = lax.rsqrt(squares * (1.0 / 4096) + EPS)
    hidden = activate(acc, scale)

    for kind in (2, 3, 4):
        w_copy(kind, 2).wait_recv()
    for k in range(4):
        lanes = pl.ds(pl.multiple_of(((zcol + k) % 4) * 1024, 1024), 1024)
        product = jnp.dot(hidden, wall[2, 0:6, :, lanes].reshape(480, 1024), preferred_element_type=F32)
        for b in range(2):
            oown[k, :, b] = product[64 * b : 64 * (b + 1)].reshape(4, 16, 1024)

    for m in range(3):
        w_copy(6, m).wait_recv()
        w_copy(5, m).start()
    for m in range(2):
        w_copy(5, m).wait_recv()
    late = [jnp.zeros((128, 160), F32), jnp.zeros((128, 160), F32)]
    for block in range(4):
        for m, product in enumerate(gate_up(block, 6, 8)):
            late[m] = late[m] + product
    hidden = activate(late, scale)

    w_copy(5, 2).wait_recv()

    def o_send(block, k, d):
        return remote(osend.at[block, (x + d) % 4], orecv.at[k, d], os_.at[k, d], or_.at[k, d], passage=peer(d, 0))

    for k in (2, 1, 3, 0):
        block = (zcol + k) % 4
        lanes = pl.ds(pl.multiple_of(block * 1024, 1024), 1024)
        product = jnp.dot(hidden, wall[2, 6:8, :, lanes].reshape(160, 1024), preferred_element_type=F32)
        for b in range(2):
            half = oown[k, :, b] + product[64 * b : 64 * (b + 1)].reshape(4, 16, 1024)
            osend[block, :, b] = half.astype(BF)
            oown[k, :, b] = half
        for d in (1, 3, 2):
            o_send(block, k, d).start()

    def f_send(o):
        to = (z + o) % 8
        return remote(fsend.at[to // 2, to % 2], frecv.at[o], fs.at[o], fr.at[o], tensor=to)

    for k in (2, 1, 3, 0):
        block = (zcol + k) % 4
        total = oown[k, x].reshape(32, 1024)
        for d in (1, 3, 2):
            o_send(block, k, d).wait_recv()
            total = total + orecv[k, d].reshape(32, 1024).astype(F32)
        fsend[block, 0] = total[:, :512].astype(BF)
        fsend[block, 1] = total[:, 512:].astype(BF)
        if k == 0:
            fown[0] = total[:, :512]
            fown[1] = total[:, 512:]
            f_send((zmate - z + 8) % 8).start()
        else:
            for e in range(2):
                f_send((2 * block + e - z + 8) % 8).start()

    mid_send.wait_recv()
    mine = mid[zpar] + fown[zpar]
    other = midr[...]
    for o in range(1, 8):
        f_send(o).wait_recv()
        if o % 2 == 0:
            mine = mine + frecv[o].astype(F32)
        else:
            other = other + frecv[o].astype(F32)
    for b in range(2):
        part = slice(16 * b, 16 * (b + 1))
        out_ref[pl.ds(pl.multiple_of(32 * b + zpar * 16, 16), 16), :] = mine[part].astype(BF)
        out_ref[pl.ds(pl.multiple_of(32 * b + 16 - zpar * 16, 16), 16), :] = other[part].astype(BF)

    for b in range(2):
        for t, dy in others:
            q_send(b, t, dy).wait_send()
            part_send(b, t, dy).wait_send()
        for t in range(4):
            q_hand(b, t).wait_send()
            half_send(4 * b + t).wait_send()
        for o in range(1, 8):
            wo_send(b, o).wait_send()
        for o in range(4):
            if o > 0:
                z_send(b, o).wait_send()
            for d in (1, 2, 3):
                x_send(b, o, d).wait_send()
    for m in range(3):
        for kind in range(7):
            w_copy(kind, m).wait_send()
    mid_send.wait_send()
    for o in range(1, 8):
        f_send(o).wait_send()
    for k in range(4):
        for d in (1, 2, 3):
            o_send((zcol + k) % 4, k, d).wait_send()


def on_device(
    answer_states, cross_keys, cross_values, passage_lengths, passage_sources, source_bias,
    query_weight, output_weight, attn_gain, ffn_gain, gate_weight, up_weight, down_weight,
):
    hbm = pl.BlockSpec(memory_space=pl.ANY)
    smem = pl.BlockSpec(memory_space=pltpu.SMEM)
    vmem = pl.BlockSpec(memory_space=pltpu.VMEM)
    dma = pltpu.SemaphoreType.DMA
    return pl.pallas_call(
        block_kernel,
        out_shape=jax.ShapeDtypeStruct((64, 512), BF),
        in_specs=[hbm, hbm, hbm, smem, smem, smem, hbm, hbm, vmem, vmem, hbm, hbm, hbm],
        out_specs=vmem,
        scratch_shapes=[
            pltpu.VMEM((64, 4096), BF),
            pltpu.VMEM((4096, 512), BF),
            pltpu.VMEM((512, 4096), BF),
            pltpu.VMEM((4, 1024, 256), BF),
            pltpu.VMEM((4, 1024, 256), BF),
            pltpu.VMEM((256, 128), BF),
            pltpu.VMEM((1536, 128), BF),
            pltpu.VMEM((128, 512), BF),
            pltpu.VMEM((2, 4, 2, 2, 32, 512), BF),
            pltpu.VMEM((8, 2, 3, 64, 512), F32),
            pltpu.VMEM((8, 3, 64, 512), F32),
            pltpu.VMEM((8, 2, 32, 640), BF),
            pltpu.VMEM((2, 4, 2, 32, 640), BF),
            pltpu.VMEM((2, 4, 2, 16, 1024), BF),
            pltpu.VMEM((2, 8, 16, 1024), BF),
            pltpu.VMEM((2, 2, 16, 1024), F32),
            pltpu.VMEM((2, 32, 512), F32),
            pltpu.VMEM((32, 512), F32),
            pltpu.VMEM((4, 2, 4, 16, 1024), BF),
            pltpu.VMEM((2, 128, 480), F32),
            pltpu.VMEM((4, 4, 2, 16, 1024), F32),
            pltpu.VMEM((4, 4, 2, 16, 1024), BF),
            pltpu.VMEM((4, 4, 2, 16, 1024), BF),
            pltpu.VMEM((2, 32, 512), F32),
            pltpu.VMEM((4, 2, 32, 512), BF),
            pltpu.VMEM((8, 32, 512), BF),
            pltpu.VMEM((3, 8, 80, 4096), BF),
            dma((13,)), dma((4,)),
            dma((7, 3)), dma((7, 3)),
            dma((2, 4, 2)), dma((2, 4, 2)), dma((2, 4)), dma((2, 4)),
            dma((8,)), dma((8,)), dma((2, 4, 2)), dma((2, 4, 2)),
            dma((2, 8)), dma((2, 8)), dma, dma,
            dma((2, 4)), dma((2, 4)), dma((2, 4, 4)), dma((2, 4, 4)),
            dma((4, 4)), dma((4, 4)), dma((8,)), dma((8,)),
        ],
        compiler_params=pltpu.CompilerParams(
            collective_id=0, has_side_effects=True, vmem_limit_bytes=60 * 1024 * 1024
        ),
        cost_estimate=pl.CostEstimate(flops=5_000_000_000, bytes_accessed=14_000_000, transcendentals=9_000_000),
        name="decoder_block",
    )(
        answer_states, cross_keys, cross_values, passage_lengths, passage_sources, source_bias.T,
        query_weight, output_weight, attn_gain.reshape(1, 4096), ffn_gain.reshape(1, 4096),
        gate_weight.T, up_weight.T, down_weight,
    )


def solution(mesh):
    return jax.shard_map(
        on_device,
        mesh=mesh,
        in_specs=(
            P(("dp", "passage"), None),
            P(("dp", "passage"), "tensor"),
            P(("dp", "passage"), "tensor"),
            P(("dp", "passage")),
            P(("dp", "passage")),
            P(None, "tensor"),
            P(None, "tensor"),
            P("tensor", None),
            P(),
            P(),
            P(None, ("tensor", "passage")),
            P(None, ("tensor", "passage")),
            P(("tensor", "passage"), None),
        ),
        out_specs=P(("dp", "passage"), "tensor"),
        check_vma=False,
    )
```

time: 96.5 us -> 92.1 us (0.954)
  the two profiles are of different devices: /device:TPU:16 before, /device:TPU:1 now
where the time goes in v2:
time: 92.1 us; the launch traced here: 91.9 us
  Pallas kernels  90.4 us (98%)
  local copies, waits for them, and re-layouts  1.47 us (2%)
    pallas_call x1, Pallas kernels, on_device(): pl.pallas_call(block_kernel, out_shape=jax.ShapeDtypeStruct((64, 512), BF...  90.4 us

profile of v2, /device:TPU:1, one launch (start us, length us, event | category | flops | bytes accessed | tf_op | source)
XLA Modules:
  0.0 91.9 jit_solution(1081551144839671134)
XLA Ops:
  0.0 90.4 %decoder_block.1 = bf16[64,512]{1,0:T(8,128)(2,1)} custom-call(bf16[64,4096]{1,0:T(8,128)(2,1)} %states_h.1, bf16[1024,512]{1,0:T(8,128)(2,1)} %keys_h.1, bf16[1024,512]{1,0:T(8,128)(2,1)} %values_h.1, s32[4]{0:T(128)} %lens_s.1, s32[4]{0:T(128)} %srcs_s.1, f32[8,32]{1,0:T(8,128)} %bitcast.9, bf16[4096,512]{1,0:T(8,128)(2,1)} %wq_h.1, ...), custom_call_target="tpu_custom_call" | custom-call | flops 5000000000 | bytes 14000000 | tf_op jit(solution)/shard_map/decoder_block/pallas_call | solution.py:499
  90.4 1.5 %copy.15 = bf16[64,512]{1,0:T(8,128)(2,1)} copy(bf16[64,512]{1,0:T(8,128)(2,1)} %decoder_block.1) | data formatting | bytes 131072

commit v3 on v2

--- a/solution.py
+++ b/solution.py
@@ -35,9 +35,9 @@
     out_ref,
     states, wq, wo, kaug, vaug, qaug, sel, expand,
     qall, ostage, srecv, rsend, rrecv,
-    wsend, wrecv, wown, mid, midr, fbuf, acc, oown, osend, orecv, fown, fsend, frecv, wall,
+    wsend, wrecv, wown, mid, midr, sq, sqin, fbuf, acc, oown, osend, orecv, fown, fsend, frecv, wall,
     load_sem, wq_sem, ws, wr, qs, qr, qfs, qfr, ss, sr, rs, rr, as_, ar, ms, mr,
-    zs, zr, xs, xr, os_, or_, fs, fr,
+    zs, zr, xs, xr, os_, or_, fs, fr, sqs, sqr,
 ):
     dp = lax.axis_index("dp")
     z = lax.axis_index("tensor")
@@ -287,7 +287,25 @@
             middle = middle + wrecv[b, o].astype(F32)
         mid[0, 16 * b : 16 * b + 16] = middle[:, :512]
         mid[1, 16 * b : 16 * b + 16] = middle[:, 512:]
-        fbuf[zcol, b, x] = (middle * fgain[:, lanes]).astype(BF)
+        square = jnp.sum(middle * middle, axis=-1, keepdims=True)
+        sq[b] = jnp.broadcast_to(square, (16, 128))
+        for o in (1, 3, 2):
+            sq_send(b, o).start()
+
+    def sq_send(b, o):
+        return remote(sq.at[b], sqin.at[b, o], sqs.at[b, o], sqr.at[b, o], tensor=(z + 2 * o) % 8)
+
+    def normalise(b):
+        square = sq[b]
+        for o in (1, 2, 3):
+            sq_send(b, o).wait_recv()
+            square = square + sqin[b, o]
+        scale = lax.rsqrt(square * (1.0 / 4096) + EPS)[:, :1]
+        for e in range(2):
+            lanes = pl.ds(pl.multiple_of(zcol * 1024 + 512 * e, 512), 512)
+            fbuf[zcol, b, x, :, 512 * e : 512 * (e + 1)] = (
+                mid[e, 16 * b : 16 * b + 16] * scale * fgain[:, lanes]
+            ).astype(BF)
         for o in (1, 3, 2):
             z_send(b, o).start()
         for d in (1, 3, 2):
@@ -351,9 +369,11 @@
     residual(0)
 
     project(1)
+    normalise(0)
     for o in (1, 3, 2):
         forward(0, o)
     residual(1)
+    normalise(1)
     mid_send = remote(mid.at[1 - zpar], midr, ms, mr, tensor=zmate)
     mid_send.start()
     for o in (1, 3, 2):
@@ -371,28 +391,23 @@
             for m in range(2)
         ]
 
-    def activate(sums, scale):
-        gate = sums[0] * scale
-        return (jax.nn.gelu(gate, approximate=True) * (sums[1] * scale)).astype(BF)
+    def activate(sums):
+        return (jax.nn.gelu(sums[0], approximate=True) * sums[1]).astype(BF)
 
     for m in range(2):
         for kind in (2, 3, 4):
             w_copy(kind, m).wait_recv()
-    squares = jnp.zeros((128, 1), F32)
     for n, o in enumerate((0, 1, 3, 2)):
         for b in range(2):
             for d in (1, 3, 2):
                 x_arrival(b, o, d).wait_recv()
         block = ((z + 8 - 2 * o) % 8) // 2
-        plain = fbuf[block].reshape(128, 1024).astype(F32) / fgain[:, pl.ds(pl.multiple_of(block * 1024, 1024), 1024)]
-        squares = squares + jnp.sum(plain * plain, axis=-1, keepdims=True)
         for m, product in enumerate(gate_up(block, 0, 6)):
             if n == 0:
                 acc[m] = product
             else:
                 acc[m] += product
-    scale = lax.rsqrt(squares * (1.0 / 4096) + EPS)
-    hidden = activate(acc, scale)
+    hidden = activate(acc)
 
     for kind in (2, 3, 4):
         w_copy(kind, 2).wait_recv()
@@ -411,7 +426,7 @@
     for block in range(4):
         for m, product in enumerate(gate_up(block, 6, 8)):
             late[m] = late[m] + product
-    hidden = activate(late, scale)
+    hidden = activate(late)
 
     w_copy(5, 2).wait_recv()
 
@@ -474,6 +489,7 @@
             wo_send(b, o).wait_send()
         for o in range(4):
             if o > 0:
+                sq_send(b, o).wait_send()
                 z_send(b, o).wait_send()
             for d in (1, 2, 3):
                 x_send(b, o, d).wait_send()
@@ -520,6 +536,8 @@
             pltpu.VMEM((2, 2, 16, 1024), F32),
             pltpu.VMEM((2, 32, 512), F32),
             pltpu.VMEM((32, 512), F32),
+            pltpu.VMEM((2, 16, 128), F32),
+            pltpu.VMEM((2, 4, 16, 128), F32),
             pltpu.VMEM((4, 2, 4, 16, 1024), BF),
             pltpu.VMEM((2, 128, 480), F32),
             pltpu.VMEM((4, 4, 2, 16, 1024), F32),
@@ -535,7 +553,7 @@
             dma((8,)), dma((8,)), dma((2, 4, 2)), dma((2, 4, 2)),
             dma((2, 8)), dma((2, 8)), dma, dma,
             dma((2, 4)), dma((2, 4)), dma((2, 4, 4)), dma((2, 4, 4)),
-            dma((4, 4)), dma((4, 4)), dma((8,)), dma((8,)),
+            dma((4, 4)), dma((4, 4)), dma((8,)), dma((8,)), dma((2, 4)), dma((2, 4)),
         ],
         compiler_params=pltpu.CompilerParams(
             collective_id=0, has_side_effects=True, vmem_limit_bytes=60 * 1024 * 1024

time: 92.1 us -> 101 us (1.097)
  Pallas kernels: 90.4 us -> 99.4 us
    pallas_call x1, Pallas kernels: 90.4 us -> 99.4 us  [on_device(): pl.pallas_call(block_kernel, out_shape=jax.ShapeDtypeStruct((64, 512), BF...]
where the time goes in v3:
time: 101 us
  Pallas kernels  99.4 us (98%)
  local copies, waits for them, and re-layouts  1.47 us (1%)
    pallas_call x1, Pallas kernels, on_device(): pl.pallas_call(block_kernel, out_shape=jax.ShapeDtypeStruct((64, 512), BF...  99.4 us

profile of v3, /device:TPU:1, one launch (start us, length us, event | category | flops | bytes accessed | tf_op | source)
XLA Modules:
  0.0 100.9 jit_solution(14300876254712823306)
XLA Ops:
  0.0 99.4 %decoder_block.1 = bf16[64,512]{1,0:T(8,128)(2,1)} custom-call(bf16[64,4096]{1,0:T(8,128)(2,1)} %states_h.1, bf16[1024,512]{1,0:T(8,128)(2,1)} %keys_h.1, bf16[1024,512]{1,0:T(8,128)(2,1)} %values_h.1, s32[4]{0:T(128)} %lens_s.1, s32[4]{0:T(128)} %srcs_s.1, f32[8,32]{1,0:T(8,128)} %bitcast.9, bf16[4096,512]{1,0:T(8,128)(2,1)} %wq_h.1, ...), custom_call_target="tpu_custom_call" | custom-call | flops 5000000000 | bytes 14000000 | tf_op jit(solution)/shard_map/decoder_block/pallas_call | solution.py:515
  99.4 1.5 %copy.15 = bf16[64,512]{1,0:T(8,128)(2,1)} copy(bf16[64,512]{1,0:T(8,128)(2,1)} %decoder_block.1) | data formatting | bytes 131072

commit v4 on v2

--- a/solution.py
+++ b/solution.py
@@ -179,12 +179,19 @@
         rows = qall[n // 4, (x + 4 - shift(n % 4)) % 4].reshape(128, 512)
         head_lane = iota((128, 128), 1) < 64
         zero = jnp.zeros((128, 128), BF)
+
+        def score(j):
+            pair = rows[:, 128 * j : 128 * (j + 1)]
+            both = jnp.concatenate([jnp.where(head_lane, pair, zero), jnp.where(head_lane, zero, pair)], axis=0)
+            both = jnp.concatenate([both, qaug[...]], axis=1)
+            return lax.dot_general(both, kaug[j], NT, preferred_element_type=F32)
+
+        following = score(0)
         for j in range(4):
             cols = slice(128 * j, 128 * (j + 1))
-            pair = rows[:, cols]
-            both = jnp.concatenate([jnp.where(head_lane, pair, zero), jnp.where(head_lane, zero, pair)], axis=0)
-            both = jnp.concatenate([both, qaug[...]], axis=1)
-            scores = lax.dot_general(both, kaug[j], NT, preferred_element_type=F32)
+            scores = following
+            if j < 3:
+                following = score(j + 1)
             peak = jnp.max(scores, axis=1, keepdims=True)
             weights = jnp.exp(scores - peak).astype(BF)
             result = jnp.dot(weights, vaug[j], preferred_element_type=F32)

time: 92.1 us -> 92.9 us (level)
  no operation moved by 1% of the time
where the time goes in v4:
time: 92.9 us; the launch traced here: 92.7 us
  Pallas kernels  91.2 us (98%)
  local copies, waits for them, and re-layouts  1.47 us (2%)
    pallas_call x1, Pallas kernels, on_device(): pl.pallas_call(block_kernel, out_shape=jax.ShapeDtypeStruct((64, 512), BF...  91.2 us

profile of v4, /device:TPU:1, one launch (start us, length us, event | category | flops | bytes accessed | tf_op | source)
XLA Modules:
  0.0 92.7 jit_solution(3264322946933184876)
XLA Ops:
  0.0 91.2 %decoder_block.1 = bf16[64,512]{1,0:T(8,128)(2,1)} custom-call(bf16[64,4096]{1,0:T(8,128)(2,1)} %states_h.1, bf16[1024,512]{1,0:T(8,128)(2,1)} %keys_h.1, bf16[1024,512]{1,0:T(8,128)(2,1)} %values_h.1, s32[4]{0:T(128)} %lens_s.1, s32[4]{0:T(128)} %srcs_s.1, f32[8,32]{1,0:T(8,128)} %bitcast.9, bf16[4096,512]{1,0:T(8,128)(2,1)} %wq_h.1, ...), custom_call_target="tpu_custom_call" | custom-call | flops 5000000000 | bytes 14000000 | tf_op jit(solution)/shard_map/decoder_block/pallas_call | solution.py:506
  91.2 1.5 %copy.15 = bf16[64,512]{1,0:T(8,128)(2,1)} copy(bf16[64,512]{1,0:T(8,128)(2,1)} %decoder_block.1) | data formatting | bytes 131072
